TPU v7x, 32 devices: a whole 2x2x4 slice. The times are simulated.
32 devices in a mesh: grp: 2 (over y), seq: 4 (over z), col: 4 (over x, core).
Axes of the slice: x: 2, y: 2, z: 4, core: 2. Of those that a mesh axis runs over, the one named last changes fastest.
Arguments:
- tokens: bfloat16 [4096, 4608], P(('grp', 'seq'), 'col'), parts along dimension 0, may hold values from -14 to 14
- norm_gain: float32 [4608], replicated, may hold values from 0.5 to 1.5
- query_weight: bfloat16 [4608, 2048], P('seq', 'col'), may hold values from -1 to 1
- key_weight: bfloat16 [4608, 1024], P('seq', 'col'), may hold values from -1 to 1
- value_weight: bfloat16 [4608, 1024], P('seq', 'col'), may hold values from -0.09375 to 0.09375
- out_weight: bfloat16 [2048, 4608], P('seq', 'col'), may hold values from -1 to 1
- positions: int32 [4096], P(('grp', 'seq')), parts along dimension 0, may hold values from 0 to 2047, as said below
Outputs:
- block_out: bfloat16 [4096, 4608], P(('grp', 'seq'), 'col'), parts along dimension 0
There are 2 independent parts, one for each index of `grp`. A program takes and returns all parts, laid end to end along the dimension named above; an argument that names none is the same for every part. Nothing has to cross between parts.
Inputs may be any that keep to these rules, and one draw needn't show every extreme that they name: Within a document positions rise by one from token to token. Exactly one document starts inside the slab, at a token of its middle half, where positions restart at 0; the document before it ends at position 2047.
All inputs are finite; a program needn't handle non-finite values.
Results may differ from a plain program's by a relative error of at most 0.012.
The roundings to bfloat16 on the way count: a program that leaves them out, or rounds other values in their place, can miss the bound.
Values may be sent and summed in bfloat16 or wider, within the bound.
A program may use at most 64 MiB of HBM per device.

v0:
```python
import jax
import jax.numpy as jnp
from jax import lax
from jax.sharding import PartitionSpec as P

KVH = 8
HD = 128
WIN = 4096
score_scale = 1.0 / 12.0
rope_base = 10000.0


def passed_along(block, axis, distance):
    devices = range(lax.axis_size(axis))
    route = [(i - distance, i) for i in devices if i - distance in devices]
    return lax.ppermute(block, axis, route)


def rms_norm(values_in, norm_gain):
    floats = values_in.astype(jnp.float32)
    square_mean = jnp.mean(floats * floats, axis=-1, keepdims=True)
    return (floats * lax.rsqrt(square_mean + 1e-06) * norm_gain).astype(jnp.bfloat16)


def rotate(heads_in, places):
    width = heads_in.shape[-1]
    half = width // 2
    inverse = jnp.exp(-jnp.log(rope_base) * jnp.arange(half, dtype=jnp.float32) * (2.0 / width))
    angle = places.astype(jnp.float32)[:, None] * inverse[None, :]
    cosine = jnp.cos(angle)[:, None, :]
    sine = jnp.sin(angle)[:, None, :]
    lower = heads_in[..., :half]
    upper = heads_in[..., half:]
    return jnp.concatenate([lower * cosine - upper * sine, upper * cosine + lower * sine], axis=-1)


def per_device(tokens, norm_gain, query_weight, key_weight, value_weight, out_weight, positions):
    tok_rows = tokens.shape[0]
    col_count = lax.axis_size("col")
    seq_count = lax.axis_size("seq")
    seq_index = lax.axis_index("seq")
    kv_local = KVH // col_count
    whole = lax.all_gather(tokens, "col", axis=1, tiled=True)
    normed = rms_norm(whole, norm_gain)
    all_places = lax.all_gather(positions, "seq", axis=0, tiled=True)
    pieces = (
        lax.all_gather(query_weight, "seq", axis=0, tiled=True),
        lax.all_gather(key_weight, "seq", axis=0, tiled=True),
        lax.all_gather(value_weight, "seq", axis=0, tiled=True),
    )
    columns = normed
    query_raw, key_raw, value_raw = tuple(
        (jnp.dot(columns, piece, preferred_element_type=jnp.float32) for piece in pieces)
    )
    queries = (
        rotate(query_raw.reshape(tok_rows, 2 * kv_local, HD), positions)
        .astype(jnp.bfloat16)
        .reshape(tok_rows, kv_local, 2, HD)
    )
    keys = (
        rotate(key_raw.reshape(tok_rows, kv_local, HD), positions)
        .astype(jnp.bfloat16)
        .reshape(tok_rows, kv_local * HD)
    )
    values = value_raw.astype(jnp.bfloat16)
    packed = jnp.stack([keys, values])
    reach = min(WIN // tok_rows, seq_count - 1)
    blocks = [packed]
    current = packed
    for step in range(reach):
        current = passed_along(current, "seq", 1)
        blocks.insert(0, current)
    window = jnp.concatenate(blocks, axis=1)
    span = (reach + 1) * tok_rows
    places_pad = jnp.concatenate([jnp.zeros((reach * tok_rows,), jnp.int32), all_places], axis=0)
    key_places = lax.dynamic_slice_in_dim(places_pad, seq_index * tok_rows, span, 0)
    key_index = (seq_index - reach) * tok_rows + jnp.arange(span, dtype=jnp.int32)
    query_index = seq_index * tok_rows + jnp.arange(tok_rows, dtype=jnp.int32)
    group = 1
    for candidate in range(1, reach + 2):
        if (reach + 1) % candidate == 0 and candidate * tok_rows <= max(512, tok_rows):
            group = candidate
    key_rows = group * tok_rows
    key_blocks = span // key_rows
    keys_blocked = window[0].reshape(key_blocks, key_rows, kv_local, HD)[::-1]
    values_blocked = window[1].reshape(key_blocks, key_rows, kv_local, HD)[::-1]
    places_blocked = key_places.reshape(key_blocks, key_rows)[::-1]
    index_blocked = key_index.reshape(key_blocks, key_rows)[::-1]

    def attend(carry, block):
        largest, total, summed = carry
        key_part, value_part, place_part, index_part = block
        scores = (
            jnp.einsum("qgeh,kgh->qgek", queries, key_part, preferred_element_type=jnp.float32)
            * score_scale
        )
        distance = query_index[:, None] - index_part[None, :]
        visible = (index_part[None, :] >= 0) & (distance >= 0) & (distance < WIN)
        visible = visible & (positions[:, None] - place_part[None, :] == distance)
        scores = jnp.where(visible[:, None, None, :], scores, -1e30)
        newest = jnp.maximum(largest, jnp.max(scores, axis=-1))
        factor = jnp.exp(largest - newest)
        weights = jnp.exp(scores - newest[..., None])
        total = total * factor + jnp.sum(weights, axis=-1)
        summed = summed * factor[..., None] + jnp.einsum(
            "qgek,kgh->qgeh",
            weights.astype(jnp.bfloat16),
            value_part,
            preferred_element_type=jnp.float32,
        )
        return ((newest, total, summed), None)

    start_state = (
        jnp.full((tok_rows, kv_local, 2), -1e30, jnp.float32),
        jnp.zeros((tok_rows, kv_local, 2), jnp.float32),
        jnp.zeros((tok_rows, kv_local, 2, HD), jnp.float32),
    )
    final_state, unused = lax.scan(
        attend, start_state, (keys_blocked, values_blocked, places_blocked, index_blocked)
    )
    attended = (
        (final_state[2] / final_state[1][..., None])
        .astype(jnp.bfloat16)
        .reshape(tok_rows, 2 * kv_local * HD)
    )
    mixed = lax.all_gather(attended, "col", axis=1, tiled=True)
    columns = mixed
    projected = jnp.dot(
        columns,
        lax.all_gather(out_weight, "seq", axis=0, tiled=True),
        preferred_element_type=jnp.float32,
    )
    return (tokens.astype(jnp.float32) + projected).astype(jnp.bfloat16)


def solution(mesh):
    return jax.shard_map(
        per_device,
        mesh=mesh,
        in_specs=(
            P(("grp", "seq"), "col"),
            P(),
            P("seq", "col"),
            P("seq", "col"),
            P("seq", "col"),
            P("seq", "col"),
            P(("grp", "seq")),
        ),
        out_specs=P(("grp", "seq"), "col"),
        check_vma=False,
    )
```

profile of v0, /device:TPU:0, one launch (start us, length us, event | category | flops | bytes accessed | tf_op | source)
XLA Modules:
  0.0 397.1 jit_solution(13647404061947721689)
XLA Ops:
  6.5 0.7 all-gather.8.cloned.1.call-update
  7.3 0.7 all-gather.10.cloned.1.call-update
  8.1 0.7 all-gather.12.cloned.1.call-update
  9.4 0.7 convert_element_type.41
  10.6 38.5 %all-gather.8.cloned.1.call-done = bf16[512,4608]{1,0:T(8,128)(2,1)} async-done(((bf16[512,1152]{1,0:T(8,128)(2,1)}), bf16[512,4608]{1,0:T(8,128)(2,1)}) %all-gather.8.cloned.1.call-update) | async-done | bytes 4718608 | tf_op jit(solution)/shard_map/all_gather | solution.py:43
  49.1 3.3 fusion.31
  52.4 48.7 %all-gather.10.cloned.1.call-done = bf16[4608,256]{1,0:T(8,128)(2,1)} async-done(((bf16[1152,256]{1,0:T(8,128)(2,1)}), bf16[4608,256]{1,0:T(8,128)(2,1)}) %all-gather.10.cloned.1.call-update) | async-done | bytes 2359312 | tf_op jit(solution)/shard_map/all_gather | solution.py:48
  101.2 4.8 %fusion.39 = f32[512,256]{0,1:T(8,128)S(1)} fusion(bf16[4608,256]{1,0:T(8,128)(2,1)} %all-gather.10.cloned.1.call-done, bf16[512,4608]{1,0:T(8,128)(2,1)} %all-gather.8.cloned.1.call-done, f32[4608]{0:T(1024)S(1)} %copy-done.5, f32[512]{0:T(512)S(1)} %add_rsqrt_fusion), kind=kOutput, calls=%fused_computation.64 | convolution fusion | flops 1217396736 | bytes 7622656 | tf_op jit(solution)/shard_map/dot_general | solution.py:53
  106.3 45.8 %all-gather.12.cloned.1.call-done = bf16[4608,256]{1,0:T(8,128)(2,1)} async-done(((bf16[1152,256]{1,0:T(8,128)(2,1)}), bf16[4608,256]{1,0:T(8,128)(2,1)}) %all-gather.12.cloned.1.call-update) | async-done | bytes 2359312 | tf_op jit(solution)/shard_map/all_gather | solution.py:49
  152.1 4.6 %fusion.35 = bf16[1,512,256]{2,1,0:T(8,128)(2,1)S(1)} fusion(bf16[4608,256]{1,0:T(8,128)(2,1)} %all-gather.12.cloned.1.call-done, bf16[512,4608]{1,0:T(8,128)(2,1)} %all-gather.8.cloned.1.call-done, f32[4608]{0:T(1024)S(1)} %copy-done.5, f32[512]{0:T(512)S(1)} %add_rsqrt_fusion), kind=kOutput, calls=%fused_computation.47 | convolution fusion | flops 1217527808 | bytes 7360512 | tf_op jit(solution)/shard_map/dot_general | solution.py:53
  156.7 1.8 collective-permute-start
  158.5 20.3 %collective-permute-done = bf16[2,512,256]{2,1,0:T(8,128)(2,1)S(1)} collective-permute-done((bf16[2,512,256]{2,1,0:T(8,128)(2,1)S(1)}, bf16[2,512,256]{2,1,0:T(8,128)(2,1)S(1)}, u32[]{:S(2)}, u32[]{:S(2)}) %collective-permute-start) | collective-permute-done | bytes 524320 | tf_op jit(solution)/shard_map/ppermute | solution.py:16
  178.9 13.4 %collective-permute-start.1 = (bf16[2,512,256]{2,1,0:T(8,128)(2,1)S(1)}, bf16[2,512,256]{2,1,0:T(8,128)(2,1)S(1)}, u32[]{:S(2)}, u32[]{:S(2)}) collective-permute-start(bf16[2,512,256]{2,1,0:T(8,128)(2,1)S(1)} %collective-permute-done), channel_id=1, source_target_pairs={{0,4},{4,8},{8,12},{1,5},{5,9},{9,13},{2,6},{6,10},{10,14},{3,7},{... | collective-permute-start | bytes 1572872 | tf_op jit(solution)/shard_map/ppermute | solution.py:16
  192.4 45.2 %all-gather = s32[4,1,512]{2,1,0:T(1,128)S(1)} all-gather(s32[1,1,512]{2,1,0:T(1,128)S(1)} %bitcast.75), channel_id=1, replica_groups=mesh['grp'=2,'seq'=4,'col'=4] {'seq'}, dimensions={0}, use_global_device_ids=true | all-gather | bytes 10240 | tf_op jit(solution)/shard_map/all_gather | solution.py:45
  237.7 1.2 rev.13
  239.6 2.1 collective-permute-start.2
  241.8 26.4 %all-gather.14.cloned.1.call-done = bf16[4608,512]{1,0:T(8,128)(2,1)} async-done(((bf16[1152,512]{1,0:T(8,128)(2,1)}), bf16[4608,512]{1,0:T(8,128)(2,1)}) %all-gather.14.cloned.1.call-update) | async-done | bytes 4718608 | tf_op jit(solution)/shard_map/all_gather | solution.py:47
  268.2 6.9 %fusion.36 = f32[512,512]{0,1:T(8,128)S(1)} fusion(bf16[4608,512]{1,0:T(8,128)(2,1)} %all-gather.14.cloned.1.call-done, bf16[512,4608]{1,0:T(8,128)(2,1)} %all-gather.8.cloned.1.call-done, f32[4608]{0:T(1024)S(1)} %copy-done.5, f32[512]{0:T(512)S(1)} %add_rsqrt_fusion), kind=kOutput, calls=%fused_computation.63 | convolution fusion | flops 2425356288 | bytes 10506240 | tf_op jit(solution)/shard_map/dot_general | solution.py:53
  276.1 1.4 maximum_maximum_fusion
  277.5 1.1 fusion.41
  279.1 1.5 reshape_squeeze.7
  280.6 2.0 copy.19
  282.6 2.2 rev.15
  284.8 47.7 %while.15 = (s32[]{:T(128)}, f32[512,2,2]{0,2,1:T(2,128)S(1)}, f32[512,2,2]{0,2,1:T(2,128)S(1)}, f32[512,2,2,128]{0,3,2,1:T(8,128)}, s32[4,512]{1,0:T(4,128)}, /...) while((s32[]{:T(128)}, f32[512,2,2]{0,2,1:T(2,128)S(1)}, ...), condition=%wide.region_4.5_spmd.clone, body=%wide.region_1.4_spmd.clone.sunk | while | flops 551300096 | bytes 33705652 | solution.py:118
  284.9 0.8 compare_reduce_fusion.2
  285.7 0.7 constant_dynamic-slice_fusion.4
  286.9 2.9 fusion.61
  289.8 3.3 fusion.63
  293.3 3.3 fusion.65
  296.6 0.7 compare_reduce_fusion.2
  297.3 0.7 constant_dynamic-slice_fusion.4
  298.6 2.9 fusion.61
  301.4 3.3 fusion.63
  304.9 3.7 fusion.65
  308.6 0.7 compare_reduce_fusion.2
  309.3 0.7 constant_dynamic-slice_fusion.4
  310.6 2.9 fusion.61
  313.4 3.3 fusion.63
  316.9 3.7 fusion.65
  320.6 0.7 compare_reduce_fusion.2
  321.3 0.7 constant_dynamic-slice_fusion.4
  322.5 2.9 fusion.61
  325.4 3.3 fusion.63
  328.9 3.7 fusion.65
  332.6 2.1 divide_convert_fusion
  334.8 26.1 %all-gather.18.cloned.1.call-done = bf16[2048,1152]{1,0:T(8,128)(2,1)} async-done(((bf16[512,1152]{1,0:T(8,128)(2,1)}), bf16[2048,1152]{1,0:T(8,128)(2,1)}) %all-gather.18.cloned.1.call-update) | async-done | bytes 4718608 | tf_op jit(solution)/shard_map/all_gather | solution.py:130
  360.8 22.5 %all-gather.16.cloned.1.call-done = bf16[512,2048]{0,1:T(8,128)(2,1)} async-done(((bf16[512,512]{0,1:T(8,128)(2,1)}), bf16[512,2048]{0,1:T(8,128)(2,1)}) %all-gather.16.cloned.1.call-update) | async-done | bytes 2097168 | tf_op jit(solution)/shard_map/all_gather | solution.py:126
  383.3 6.9 %fusion.34 = bf16[512,1152]{1,0:T(8,128)(2,1)} fusion(bf16[512,2048]{0,1:T(8,128)(2,1)} %all-gather.16.cloned.1.call-done, bf16[2048,1152]{1,0:T(8,128)(2,1)} %all-gather.18.cloned.1.call-done, bf16[512,1152]{1,0:T(8,128)(2,1)S(1)} %copy-done.1), kind=kOutput, calls=%fused_computation.44 | convolution fusion | flops 2417688576 | bytes 9175040 | tf_op jit(solution)/shard_map/dot_general | solution.py:128
  (71 shorter events, 6.8 us)
Async XLA Ops:
  6.5 42.6 %all-gather.8.cloned.1.call-start = ((), (), s32[]{:S(2)}) async-start(), calls=%async_computation | async-start | bytes 5898240 | tf_op jit(solution)/shard_map/all_gather | solution.py:43
  6.5 94.6 %copy-start.5 = (f32[4608]{0:T(1024)S(1)}, f32[4608]{0:T(1024)}, u32[]{:S(2)}) copy-start(f32[4608]{0:T(1024)} %param.10) | copy-start | bytes 55300
  7.3 93.9 %all-gather.10.cloned.1.call-start = ((), (), s32[]{:S(2)}) async-start(), calls=%async_computation.1 | async-start | bytes 2949120 | tf_op jit(solution)/shard_map/all_gather | solution.py:48
  8.0 144.1 %all-gather.12.cloned.1.call-start = ((), (), s32[]{:S(2)}) async-start(), calls=%async_computation.2 | async-start | bytes 2949120 | tf_op jit(solution)/shard_map/all_gather | solution.py:49
  8.7 259.4 %all-gather.14.cloned.1.call-start = ((), (), s32[]{:S(2)}) async-start(), calls=%async_computation.3 | async-start | bytes 5898240 | tf_op jit(solution)/shard_map/all_gather | solution.py:47
  9.3 351.5 %all-gather.18.cloned.1.call-start = ((), (), s32[]{:S(2)}) async-start(), calls=%async_computation.5 | async-start | bytes 5898240 | tf_op jit(solution)/shard_map/all_gather | solution.py:130
  106.3 86.1 %copy-start.3 = (s32[512]{0:T(512)S(1)}, s32[512]{0:T(512)}, u32[]{:S(2)}) copy-start(s32[512]{0:T(512)} %param.15) | copy-start | bytes 6148
  156.7 22.1 %collective-permute-start = (bf16[2,512,256]{2,1,0:T(8,128)(2,1)S(1)}, bf16[2,512,256]{2,1,0:T(8,128)(2,1)S(1)}, u32[]{:S(2)}, u32[]{:S(2)}) collective-permute-start(bf16[2,512,256]{2,1,0:T(8,128)(2,1)S(1)} %pad_maximum_fusion), channel_id=1, source_target_pairs={{0,4},{4,8},{8,12},{1,5},{5,9},{9,13},{2,6},{6,10},{10,14},{3,7},{... | collective-permute-start | bytes 1572872 | tf_op jit(solution)/shard_map/ppermute | solution.py:16
  178.9 60.8 %collective-permute-start.1 = (bf16[2,512,256]{2,1,0:T(8,128)(2,1)S(1)}, bf16[2,512,256]{2,1,0:T(8,128)(2,1)S(1)}, u32[]{:S(2)}, u32[]{:S(2)}) collective-permute-start(bf16[2,512,256]{2,1,0:T(8,128)(2,1)S(1)} %collective-permute-done), channel_id=1, source_target_pairs={{0,4},{4,8},{8,12},{1,5},{5,9},{9,13},{2,6},{6,10},{10,14},{3,7},{... | collective-permute-start | bytes 1572872 | tf_op jit(solution)/shard_map/ppermute | solution.py:16
  192.3 191.0 %all-gather.16.cloned.1.call-start = ((), (), s32[]{:S(2)}) async-start(), calls=%async_computation.4 | async-start | bytes 2621440 | tf_op jit(solution)/shard_map/all_gather | solution.py:126
  239.6 36.5 %collective-permute-start.2 = (bf16[2,512,256]{2,1,0:T(8,128)(2,1)S(1)}, bf16[2,512,256]{2,1,0:T(8,128)(2,1)}, u32[]{:S(2)}, u32[]{:S(2)}) collective-permute-start(bf16[2,512,256]{2,1,0:T(8,128)(2,1)S(1)} %collective-permute-done.1), channel_id=1, source_target_pairs={{0,4},{4,8},{8,12},{1,5},{5,9},{9,13},{2,6},{6,10},{10,14},{3,7},{... | collective-permute-start | bytes 1572872 | tf_op jit(solution)/shard_map/ppermute | solution.py:16
  279.0 5.8 %copy-start.2 = (f32[512,2,2]{0,2,1:T(2,128)S(1)}, f32[512,2,2]{0,2,1:T(2,128)}, u32[]{:S(2)}) copy-start(f32[512,2,2]{0,2,1:T(2,128)} %custom-call.1) | copy-start | bytes 24580
  279.1 5.8 %copy-start.4 = (s32[512]{0:T(512)S(1)}, s32[512]{0:T(512)}, u32[]{:S(2)}) copy-start(s32[512]{0:T(512)} %param.15) | copy-start | bytes 6148
  284.8 98.5 %copy-start.1 = (bf16[512,1152]{1,0:T(8,128)(2,1)S(1)}, bf16[512,1152]{1,0:T(8,128)(2,1)}, u32[]{:S(2)}) copy-start(bf16[512,1152]{1,0:T(8,128)(2,1)} %param.9) | copy-start | bytes 3538948
  289.8 3.5 copy-start
  301.4 3.4 copy-start
  313.4 3.5 copy-start
  325.4 3.5 copy-start
Sparse Core Ops, SparseCore 0:
  8.9 40.1 all-gather.7
  50.7 50.4 all-gather.9
  102.8 49.2 all-gather.11
  153.5 114.6 all-gather.13
  269.6 91.2 all-gather.17
  362.3 21.0 all-gather.15
where the time goes:
time: 398 us; the launch traced here: 397 us
  waiting for transfers between devices  231 us (58%)
  matrix products  49.1 us (12%)
  blocking collectives  45.2 us (11%)
  other arithmetic  27.5 us (7%)
  starting transfers between devices  17.5 us (4%)
  between operations  13.7 us (3%)
  local copies, waits for them, and re-layouts  12.9 us (3%)
    all_gather x1, waiting for transfers between devices, per_device(): lax.all_gather(key_weight, 'seq', axis=0, tiled=True)  48.7 us
    all_gather x1, waiting for transfers between devices, per_device(): lax.all_gather(value_weight, 'seq', axis=0, tiled=True)  45.8 us
    all_gather x1, blocking collectives, per_device(): all_places = lax.all_gather(positions, 'seq', axis=0, tiled=True)  45.2 us
    all_gather x1, waiting for transfers between devices, per_device(): whole = lax.all_gather(tokens, 'col', axis=1, tiled=True)  38.5 us
    all_gather x1, waiting for transfers between devices, per_device(): lax.all_gather(query_weight, 'seq', axis=0, tiled=True)  26.4 us
    all_gather x1, waiting for transfers between devices, per_device(): lax.all_gather(out_weight, 'seq', axis=0, tiled=True)  26.1 us
    all_gather x1, waiting for transfers between devices, per_device(): mixed = lax.all_gather(attended, 'col', axis=1, tiled=True)  22.5 us
    ppermute x3, waiting for transfers between devices, passed_along(): return lax.ppermute(block, axis, route)  20.3 us
  transfers between devices with their start and end apart: 9, of which 7 were waited for; matrix products, arithmetic and copies ran while one was open for 21% of the time, Pallas kernels for 0%

commit v1 on v0

--- a/solution.py
+++ b/solution.py
@@ -8,6 +8,18 @@
 WIN = 4096
 score_scale = 1.0 / 12.0
 rope_base = 10000.0
+
+
+def collect(value, axis, dim):
+    ways, here = (lax.axis_size(axis), lax.axis_index(axis))
+    grown, reach = (value, 1)
+    while reach < ways:
+        theirs = lax.ppermute(grown, axis, [(d, d ^ reach) for d in range(ways)])
+        mine_first = jnp.concatenate([grown, theirs], axis=dim)
+        theirs_first = jnp.concatenate([theirs, grown], axis=dim)
+        grown = jnp.where(here & reach == 0, mine_first, theirs_first)
+        reach = 2 * reach
+    return grown
 
 
 def passed_along(block, axis, distance):
@@ -46,7 +58,7 @@
     pieces = (
         lax.all_gather(query_weight, "seq", axis=0, tiled=True),
         lax.all_gather(key_weight, "seq", axis=0, tiled=True),
-        lax.all_gather(value_weight, "seq", axis=0, tiled=True),
+        collect(value_weight, "seq", 0),
     )
     columns = normed
     query_raw, key_raw, value_raw = tuple(

time: 398 us -> 367 us (0.922)
  waiting for transfers between devices: 231 us -> 190 us
  starting transfers between devices: 17.5 us -> 26.5 us
    all_gather x1 -> x0, waiting for transfers between devices: 45.8 us -> none  [per_device(): lax.all_gather(value_weight, 'seq', axis=0, tiled=True)]
    all_gather x1, waiting for transfers between devices: 38.5 us -> 19.3 us  [per_device(): whole = lax.all_gather(tokens, 'col', axis=1, tiled=True)]
    all_gather x1, waiting for transfers between devices: 48.7 us -> 66.9 us  [per_device(): lax.all_gather(key_weight, 'seq', axis=0, tiled=True)]
    ppermute x0 -> x2, waiting for transfers between devices: none -> 12.3 us  [collect(): theirs = lax.ppermute(grown, axis, [(d, d ^ reach) for d in range(ways)])]
    all_gather x1, waiting for transfers between devices: 26.4 us -> 19.3 us  [per_device(): lax.all_gather(query_weight, 'seq', axis=0, tiled=True)]
    ppermute x0 -> x2, starting transfers between devices: none -> 5.9 us  [collect(): theirs = lax.ppermute(grown, axis, [(d, d ^ reach) for d in range(ways)])]
  transfers between devices with their start and end apart: 9 -> 10, of which waited for: 7 -> 7; matrix products, arithmetic and copies ran while one was open for 21% -> 23% of each run, Pallas kernels for 0% -> 0%
where the time goes in v1:
time: 367 us; the launch traced here: 366 us
  waiting for transfers between devices  190 us (52%)
  matrix products  49.5 us (13%)
  blocking collectives  44.5 us (12%)
  other arithmetic  29.1 us (8%)
  starting transfers between devices  26.5 us (7%)
  between operations  13.4 us (4%)
  local copies, waits for them, and re-layouts  13 us (4%)
    all_gather x1, waiting for transfers between devices, per_device(): lax.all_gather(key_weight, 'seq', axis=0, tiled=True)  66.9 us
    all_gather x1, blocking collectives, per_device(): all_places = lax.all_gather(positions, 'seq', axis=0, tiled=True)  44.5 us
    all_gather x1, waiting for transfers between devices, per_device(): lax.all_gather(out_weight, 'seq', axis=0, tiled=True)  24.5 us
    ppermute x3, waiting for transfers between devices, passed_along(): return lax.ppermute(block, axis, route)  23.2 us
    all_gather x1, waiting for transfers between devices, per_device(): mixed = lax.all_gather(attended, 'col', axis=1, tiled=True)  22.5 us
    ppermute x3, starting transfers between devices, passed_along(): return lax.ppermute(block, axis, route)  20.4 us
    all_gather x1, waiting for transfers between devices, per_device(): whole = lax.all_gather(tokens, 'col', axis=1, tiled=True)  19.3 us
    all_gather x1, waiting for transfers between devices, per_device(): lax.all_gather(query_weight, 'seq', axis=0, tiled=True)  19.3 us
  transfers between devices with their start and end apart: 10, of which 7 were waited for; matrix products, arithmetic and copies ran while one was open for 23% of the time, Pallas kernels for 0%

profile of v1, /device:TPU:0, one launch (start us, length us, event | category | flops | bytes accessed | tf_op | source)
XLA Modules:
  0.0 366.0 jit_solution(17215651380463235871)
XLA Ops:
  6.5 0.7 all-gather.7.cloned.1.call-update
  8.8 3.1 collective-permute-start
  13.1 12.3 %collective-permute-done = bf16[1152,256]{1,0:T(8,128)(2,1)S(1)} collective-permute-done((bf16[1152,256]{1,0:T(8,128)(2,1)}, bf16[1152,256]{1,0:T(8,128)(2,1)S(1)}, u32[]{:S(2)}, u32[]{:S(2)}) %collective-permute-start) | collective-permute-done | bytes 589856 | tf_op jit(solution)/shard_map/ppermute | solution.py:17
  25.4 1.5 maximum_select_fusion.4
  27.0 2.8 collective-permute-start.1
  29.8 19.3 %all-gather.7.cloned.1.call-done = bf16[512,4608]{1,0:T(8,128)(2,1)} async-done(((bf16[512,1152]{1,0:T(8,128)(2,1)}), bf16[512,4608]{1,0:T(8,128)(2,1)}) %all-gather.7.cloned.1.call-update) | async-done | bytes 4718608 | tf_op jit(solution)/shard_map/all_gather | solution.py:55
  49.1 3.3 fusion.31
  52.4 66.9 %all-gather.9.cloned.1.call-done = bf16[4608,256]{1,0:T(8,128)(2,1)} async-done(((bf16[1152,256]{1,0:T(8,128)(2,1)}), bf16[4608,256]{1,0:T(8,128)(2,1)}) %all-gather.9.cloned.1.call-update) | async-done | bytes 2359312 | tf_op jit(solution)/shard_map/all_gather | solution.py:60
  119.3 4.8 %fusion.48 = f32[512,256]{0,1:T(8,128)S(1)} fusion(bf16[4608,256]{1,0:T(8,128)(2,1)} %all-gather.9.cloned.1.call-done, bf16[512,4608]{1,0:T(8,128)(2,1)} %all-gather.7.cloned.1.call-done, f32[4608]{0:T(1024)S(1)} %copy-done.5, f32[512]{0:T(512)S(1)} %add_rsqrt_fusion), kind=kOutput, calls=%fused_computation.74 | convolution fusion | flops 1217396736 | bytes 7622656 | tf_op jit(solution)/shard_map/dot_general | solution.py:65
  124.4 4.9 %fusion.43 = bf16[1,512,256]{2,1,0:T(8,128)(2,1)S(1)} fusion(bf16[2304,256]{1,0:T(8,128)(2,1)} %collective-permute-done.1, bf16[2304,256]{1,0:T(8,128)(2,1)S(1)} %maximum_select_fusion.4, pred[]{:T(512)S(6)} %eq.13, bf16[512,4608]{1,0:T(8,128)(2,1)} %all-gather.7.cloned.1.call-done, f32[4608]{0:T(1024)S(1)} %copy-done.5, f32[512]{0:T(512)S(1)} %add_rsqrt_fusion), kind=kOutput, calls=%fused_computation.56 | convolution fusion | flops 1228144640 | bytes 7360513 | tf_op jit(solution)/shard_map/dot_general | solution.py:65
  129.4 1.3 collective-permute-start.2
  130.8 23.2 %collective-permute-done.2 = bf16[2,512,256]{2,1,0:T(8,128)(2,1)S(1)} collective-permute-done((bf16[2,512,256]{2,1,0:T(8,128)(2,1)S(1)}, bf16[2,512,256]{2,1,0:T(8,128)(2,1)S(1)}, u32[]{:S(2)}, u32[]{:S(2)}) %collective-permute-start.2) | collective-permute-done | bytes 524320 | tf_op jit(solution)/shard_map/ppermute | solution.py:28
  153.9 14.2 %collective-permute-start.3 = (bf16[2,512,256]{2,1,0:T(8,128)(2,1)S(1)}, bf16[2,512,256]{2,1,0:T(8,128)(2,1)S(1)}, u32[]{:S(2)}, u32[]{:S(2)}) collective-permute-start(bf16[2,512,256]{2,1,0:T(8,128)(2,1)S(1)} %collective-permute-done.2), channel_id=1, source_target_pairs={{0,4},{4,8},{8,12},{1,5},{5,9},{9,13},{2,6},{6,10},{10,14},{3,7},{... | collective-permute-start | bytes 1572872 | tf_op jit(solution)/shard_map/ppermute | solution.py:28
  168.2 44.5 %all-gather = s32[4,1,512]{2,1,0:T(1,128)S(1)} all-gather(s32[1,1,512]{2,1,0:T(1,128)S(1)} %bitcast.74), channel_id=1, replica_groups=mesh['grp'=2,'seq'=4,'col'=4] {'seq'}, dimensions={0}, use_global_device_ids=true | all-gather | bytes 10240 | tf_op jit(solution)/shard_map/all_gather | solution.py:57
  212.8 1.2 rev.13
  214.7 4.9 %collective-permute-start.4 = (bf16[2,512,256]{2,1,0:T(8,128)(2,1)S(1)}, bf16[2,512,256]{2,1,0:T(8,128)(2,1)}, u32[]{:S(2)}, u32[]{:S(2)}) collective-permute-start(bf16[2,512,256]{2,1,0:T(8,128)(2,1)S(1)} %collective-permute-done.3), channel_id=1, source_target_pairs={{0,4},{4,8},{8,12},{1,5},{5,9},{9,13},{2,6},{6,10},{10,14},{3,7},{... | collective-permute-start | bytes 1572872 | tf_op jit(solution)/shard_map/ppermute | solution.py:28
  219.6 19.3 %all-gather.11.cloned.1.call-done = bf16[4608,512]{1,0:T(8,128)(2,1)} async-done(((bf16[1152,512]{1,0:T(8,128)(2,1)}), bf16[4608,512]{1,0:T(8,128)(2,1)}) %all-gather.11.cloned.1.call-update) | async-done | bytes 4718608 | tf_op jit(solution)/shard_map/all_gather | solution.py:59
  238.9 6.9 %fusion.45 = f32[512,512]{0,1:T(8,128)S(1)} fusion(bf16[4608,512]{1,0:T(8,128)(2,1)} %all-gather.11.cloned.1.call-done, bf16[512,4608]{1,0:T(8,128)(2,1)} %all-gather.7.cloned.1.call-done, f32[4608]{0:T(1024)S(1)} %copy-done.5, f32[512]{0:T(512)S(1)} %add_rsqrt_fusion), kind=kOutput, calls=%fused_computation.73 | convolution fusion | flops 2425356288 | bytes 10506240 | tf_op jit(solution)/shard_map/dot_general | solution.py:65
  246.8 1.4 maximum_maximum_fusion
  248.2 1.1 fusion.50
  249.9 1.4 reshape_squeeze.7
  251.3 2.0 copy.19
  253.3 2.3 rev.15
  255.6 47.9 %while.15 = (s32[]{:T(128)}, f32[512,2,2]{0,2,1:T(2,128)S(1)}, f32[512,2,2]{0,2,1:T(2,128)S(1)}, f32[512,2,2,128]{0,3,2,1:T(8,128)}, s32[4,512]{1,0:T(4,128)}, /...) while((s32[]{:T(128)}, f32[512,2,2]{0,2,1:T(2,128)S(1)}, ...), condition=%wide.region_4.5_spmd.clone, body=%wide.region_1.4_spmd.clone.sunk | while | flops 551300096 | bytes 33705652 | solution.py:130
  255.6 0.8 compare_reduce_fusion.2
  256.4 0.7 constant_dynamic-slice_fusion.4
  257.7 2.9 fusion.69
  260.5 3.3 fusion.71
  264.1 3.3 fusion.73
  267.4 0.7 compare_reduce_fusion.2
  268.1 0.7 constant_dynamic-slice_fusion.4
  269.4 2.9 fusion.69
  272.2 3.3 fusion.71
  275.7 3.7 %fusion.73 = f32[512,2,2,128]{0,3,2,1:T(8,128)} fusion(f32[2,512,512,2]{2,1,3,0:T(8,128)S(1)} %copy-done, f32[512,2,2]{0,2,1:T(2,128)S(1)} %fusion.70, pred[512,512]{0,1:T(8,128)(4,1)S(1)} %fusion.68, f32[512,2,2,128]{0,3,2,1:T(8,128)} %get-tuple-element.235, f32[512,2,2]{0,2,1:T(2,128)S(1)} %get-tuple-element.218, pred[]{:T(512)S(6)} %compare.4, ...), kind=kOutput, calls=%fused_computation.15.clone.1 | convolution fusion | flops 273416192 | bytes 6832641 | tf_op jit(solution)/shard_map/while/body/eval_jaxpr/qgek,kgh->qgeh/dot_general | solution.py:117
  279.4 0.7 compare_reduce_fusion.2
  280.2 0.7 constant_dynamic-slice_fusion.4
  281.4 2.9 fusion.69
  284.3 3.3 fusion.71
  287.8 3.7 %fusion.73 = f32[512,2,2,128]{0,3,2,1:T(8,128)} fusion(f32[2,512,512,2]{2,1,3,0:T(8,128)S(1)} %copy-done, f32[512,2,2]{0,2,1:T(2,128)S(1)} %fusion.70, pred[512,512]{0,1:T(8,128)(4,1)S(1)} %fusion.68, f32[512,2,2,128]{0,3,2,1:T(8,128)} %get-tuple-element.235, f32[512,2,2]{0,2,1:T(2,128)S(1)} %get-tuple-element.218, pred[]{:T(512)S(6)} %compare.4, ...), kind=kOutput, calls=%fused_computation.15.clone.1 | convolution fusion | flops 273416192 | bytes 6832641 | tf_op jit(solution)/shard_map/while/body/eval_jaxpr/qgek,kgh->qgeh/dot_general | solution.py:117
  291.5 0.7 compare_reduce_fusion.2
  292.2 0.7 constant_dynamic-slice_fusion.4
  293.4 2.9 fusion.69
  296.3 3.3 fusion.71
  299.8 3.7 %fusion.73 = f32[512,2,2,128]{0,3,2,1:T(8,128)} fusion(f32[2,512,512,2]{2,1,3,0:T(8,128)S(1)} %copy-done, f32[512,2,2]{0,2,1:T(2,128)S(1)} %fusion.70, pred[512,512]{0,1:T(8,128)(4,1)S(1)} %fusion.68, f32[512,2,2,128]{0,3,2,1:T(8,128)} %get-tuple-element.235, f32[512,2,2]{0,2,1:T(2,128)S(1)} %get-tuple-element.218, pred[]{:T(512)S(6)} %compare.4, ...), kind=kOutput, calls=%fused_computation.15.clone.1 | convolution fusion | flops 273416192 | bytes 6832641 | tf_op jit(solution)/shard_map/while/body/eval_jaxpr/qgek,kgh->qgeh/dot_general | solution.py:117
  303.5 2.1 divide_convert_fusion
  305.6 24.5 %all-gather.15.cloned.1.call-done = bf16[2048,1152]{1,0:T(8,128)(2,1)} async-done(((bf16[512,1152]{1,0:T(8,128)(2,1)}), bf16[2048,1152]{1,0:T(8,128)(2,1)}) %all-gather.15.cloned.1.call-update) | async-done | bytes 4718608 | tf_op jit(solution)/shard_map/all_gather | solution.py:142
  330.1 22.5 %all-gather.13.cloned.1.call-done = bf16[512,2048]{0,1:T(8,128)(2,1)} async-done(((bf16[512,512]{0,1:T(8,128)(2,1)}), bf16[512,2048]{0,1:T(8,128)(2,1)}) %all-gather.13.cloned.1.call-update) | async-done | bytes 2097168 | tf_op jit(solution)/shard_map/all_gather | solution.py:138
  352.6 6.9 %fusion.34 = bf16[512,1152]{1,0:T(8,128)(2,1)} fusion(bf16[512,2048]{0,1:T(8,128)(2,1)} %all-gather.13.cloned.1.call-done, bf16[2048,1152]{1,0:T(8,128)(2,1)} %all-gather.15.cloned.1.call-done, bf16[512,1152]{1,0:T(8,128)(2,1)S(1)} %copy-done.1), kind=kOutput, calls=%fused_computation.44 | convolution fusion | flops 2417688576 | bytes 9175040 | tf_op jit(solution)/shard_map/dot_general | solution.py:140
  (73 shorter events, 8.4 us)
Async XLA Ops:
  6.5 42.6 %all-gather.7.cloned.1.call-start = ((), (), s32[]{:S(2)}) async-start(), calls=%async_computation | async-start | bytes 5898240 | tf_op jit(solution)/shard_map/all_gather | solution.py:55
  7.3 112.0 %all-gather.9.cloned.1.call-start = ((), (), s32[]{:S(2)}) async-start(), calls=%async_computation.1 | async-start | bytes 2949120 | tf_op jit(solution)/shard_map/all_gather | solution.py:60
  8.0 111.3 %copy-start.5 = (f32[4608]{0:T(1024)S(1)}, f32[4608]{0:T(1024)}, u32[]{:S(2)}) copy-start(f32[4608]{0:T(1024)} %param.10) | copy-start | bytes 55300
  8.0 230.9 %all-gather.11.cloned.1.call-start = ((), (), s32[]{:S(2)}) async-start(), calls=%async_computation.2 | async-start | bytes 5898240 | tf_op jit(solution)/shard_map/all_gather | solution.py:59
  8.8 321.3 %all-gather.15.cloned.1.call-start = ((), (), s32[]{:S(2)}) async-start(), calls=%async_computation.4 | async-start | bytes 5898240 | tf_op jit(solution)/shard_map/all_gather | solution.py:142
  8.8 16.6 %collective-permute-start = (bf16[1152,256]{1,0:T(8,128)(2,1)}, bf16[1152,256]{1,0:T(8,128)(2,1)S(1)}, u32[]{:S(2)}, u32[]{:S(2)}) collective-permute-start(bf16[1152,256]{1,0:T(8,128)(2,1)} %param.13), channel_id=1, source_target_pairs={{0,4},{4,0},{8,12},{12,8},{1,5},{5,1},{9,13},{13,9},{2,6},{6,2},{1... | collective-permute-start | bytes 1769480 | tf_op jit(solution)/shard_map/ppermute | solution.py:17
  27.0 97.4 %collective-permute-start.1 = (bf16[2304,256]{1,0:T(8,128)(2,1)S(1)}, bf16[2304,256]{1,0:T(8,128)(2,1)}, u32[]{:S(2)}, u32[]{:S(2)}) collective-permute-start(bf16[2304,256]{1,0:T(8,128)(2,1)S(1)} %maximum_select_fusion.4), channel_id=1, source_target_pairs={{0,8},{4,12},{8,0},{12,4},{1,9},{5,13},{9,1},{13,5},{2,10},{6,14},... | collective-permute-start | bytes 3538952 | tf_op jit(solution)/shard_map/ppermute | solution.py:17
  124.4 43.8 %copy-start.3 = (s32[512]{0:T(512)S(1)}, s32[512]{0:T(512)}, u32[]{:S(2)}) copy-start(s32[512]{0:T(512)} %param.15) | copy-start | bytes 6148
  129.4 24.5 %collective-permute-start.2 = (bf16[2,512,256]{2,1,0:T(8,128)(2,1)S(1)}, bf16[2,512,256]{2,1,0:T(8,128)(2,1)S(1)}, u32[]{:S(2)}, u32[]{:S(2)}) collective-permute-start(bf16[2,512,256]{2,1,0:T(8,128)(2,1)S(1)} %pad_maximum_fusion), channel_id=1, source_target_pairs={{0,4},{4,8},{8,12},{1,5},{5,9},{9,13},{2,6},{6,10},{10,14},{3,7},{... | collective-permute-start | bytes 1572872 | tf_op jit(solution)/shard_map/ppermute | solution.py:28
  153.9 60.8 %collective-permute-start.3 = (bf16[2,512,256]{2,1,0:T(8,128)(2,1)S(1)}, bf16[2,512,256]{2,1,0:T(8,128)(2,1)S(1)}, u32[]{:S(2)}, u32[]{:S(2)}) collective-permute-start(bf16[2,512,256]{2,1,0:T(8,128)(2,1)S(1)} %collective-permute-done.2), channel_id=1, source_target_pairs={{0,4},{4,8},{8,12},{1,5},{5,9},{9,13},{2,6},{6,10},{10,14},{3,7},{... | collective-permute-start | bytes 1572872 | tf_op jit(solution)/shard_map/ppermute | solution.py:28
  168.1 184.4 %all-gather.13.cloned.1.call-start = ((), (), s32[]{:S(2)}) async-start(), calls=%async_computation.3 | async-start | bytes 2621440 | tf_op jit(solution)/shard_map/all_gather | solution.py:138
  214.7 32.1 %collective-permute-start.4 = (bf16[2,512,256]{2,1,0:T(8,128)(2,1)S(1)}, bf16[2,512,256]{2,1,0:T(8,128)(2,1)}, u32[]{:S(2)}, u32[]{:S(2)}) collective-permute-start(bf16[2,512,256]{2,1,0:T(8,128)(2,1)S(1)} %collective-permute-done.3), channel_id=1, source_target_pairs={{0,4},{4,8},{8,12},{1,5},{5,9},{9,13},{2,6},{6,10},{10,14},{3,7},{... | collective-permute-start | bytes 1572872 | tf_op jit(solution)/shard_map/ppermute | solution.py:28
  249.8 5.8 %copy-start.2 = (f32[512,2,2]{0,2,1:T(2,128)S(1)}, f32[512,2,2]{0,2,1:T(2,128)}, u32[]{:S(2)}) copy-start(f32[512,2,2]{0,2,1:T(2,128)} %custom-call.1) | copy-start | bytes 24580
  249.8 5.8 %copy-start.4 = (s32[512]{0:T(512)S(1)}, s32[512]{0:T(512)}, u32[]{:S(2)}) copy-start(s32[512]{0:T(512)} %param.15) | copy-start | bytes 6148
  255.6 97.0 %copy-start.1 = (bf16[512,1152]{1,0:T(8,128)(2,1)S(1)}, bf16[512,1152]{1,0:T(8,128)(2,1)}, u32[]{:S(2)}) copy-start(bf16[512,1152]{1,0:T(8,128)(2,1)} %param.9) | copy-start | bytes 3538948
  260.5 3.5 copy-start
  272.2 3.5 copy-start
  284.3 3.5 copy-start
  296.3 3.5 copy-start
Sparse Core Ops, SparseCore 0:
  8.9 40.1 all-gather.6
  50.7 68.6 all-gather.8
  120.9 117.9 all-gather.10
  240.3 89.7 all-gather.14
  331.5 21.0 all-gather.12
